TPU v7x, 128 devices: a whole 4x4x4 slice. The times are simulated.
128 devices in a mesh: dp: 16 (over x_hi, z, core), seq: 8 (over y, x_lo).
Axes of the slice: x: 4 (x_hi: 2, x_lo: 2; x = x_hi * 2 + x_lo), y: 4, z: 4, core: 2. Of those that a mesh axis runs over, the one named last changes fastest.
Arguments:
- tokens: bfloat16 [16, 1024, 1024], P('dp', 'seq'), may hold values from -8 to 8
- memory: bfloat16 [16, 1024, 1024], P('dp', 'seq'), may hold values from -6 to 6
- cotangent: bfloat16 [16, 1024, 1024], P('dp', 'seq'), may hold values from -6 to 6
- offsets: int32 [16, 16], P('dp'), may hold values from 0 to 1023, as said below
- memory_ids: int32 [16, 1024], P('dp'), may hold values from 0 to 15, as said below
- pair_map: int32 [16, 16], P('dp'), may hold values from 0 to 15, as said below
- self_qkv: bfloat16 [1024, 3072], replicated, may hold values from -0.1875 to 0.1875
- self_out: bfloat16 [1024, 1024], replicated, may hold values from -1 to 1
- cross_query: bfloat16 [1024, 1024], replicated, may hold values from -0.1875 to 0.1875
- cross_kv: bfloat16 [1024, 2048], replicated, may hold values from -0.1875 to 0.1875
- cross_out: bfloat16 [1024, 1024], replicated, may hold values from -1 to 1
- expand_weight: bfloat16 [1024, 4096], replicated, may hold values from -0.1875 to 0.1875
- expand_bias: float32 [4096], replicated, may hold values from -1.75 to 1.75
- reduce_weight: bfloat16 [4096, 1024], replicated, may hold values from -0.09375 to 0.09375
- norm_gains: float32 [3, 1024], replicated, may hold values from 0.25 to 1.75
- bias_rows: float32 [10, 1024], replicated, may hold values from -1.75 to 1.75
Outputs:
- output: bfloat16 [16, 1024, 1024], P('dp', 'seq')
- grad_tokens: float32 [16, 1024, 1024], P('dp', 'seq')
- grad_memory: float32 [16, 1024, 1024], P('dp', 'seq')
- grad_self_qkv: float32 [1024, 3072], P('dp')
- grad_self_out: float32 [1024, 1024], P('dp')
- grad_cross_query: float32 [1024, 1024], P('dp')
- grad_cross_kv: float32 [1024, 2048], P('dp')
- grad_cross_out: float32 [1024, 1024], P('dp')
- grad_expand_weight: float32 [1024, 4096], P('dp')
- grad_expand_bias: float32 [4096], P('dp')
- grad_reduce_weight: float32 [4096, 1024], P('dp')
- grad_norm_gains: float32 [3, 1024], P(None, 'dp')
- grad_bias_rows: float32 [10, 1024], P(None, 'dp')
Inputs may be any that keep to these rules, and one draw needn't show every extreme that they name: In each row the offsets start at 0 and rise strictly; target segment s covers the positions from offsets[s] up to the next offset minus one, the last up to 1023. `memory_ids`: along each row the ids never fall, and every id from 0 to 15 appears. `pair_map`: each row is a permutation of 0 to 15.
All inputs are finite; a program needn't handle non-finite values.
Results may differ from a plain program's by a relative error of at most 0.025.
Values may be sent and summed in bfloat16 or wider, within the bound.
A program may use at most 192 MiB of HBM per device.

v0:
```python
import functools
import math

import jax
import jax.numpy as jnp
from jax import lax
from jax.experimental import pallas as pl
from jax.experimental.pallas import tpu as pltpu
from jax.sharding import PartitionSpec as P

HEADS = 16
HEAD_DIM = 64
WIDTH = 1024
TOK = 128
ROW = 1024
FF = 4096
SEQ = 8
DP = 16
PAIR = 128
NEG_FILL = -1e30
EPS = 1e-05
SCALE = HEAD_DIM ** (-0.5)
LOW = jnp.bfloat16
F32 = jnp.float32
MESH = pl.DeviceIdType.MESH
MIB = 2**20


def dot(left, right):
    return lax.dot_general(left, right, (((1,), (0,)), ((), ())), preferred_element_type=F32)


def dot_nt(left, right):
    return lax.dot_general(left, right, (((1,), (1,)), ((), ())), preferred_element_type=F32)


def dot_tn(left, right):
    return lax.dot_general(left, right, (((0,), (0,)), ((), ())), preferred_element_type=F32)


def norm_unit(values):
    average = jnp.mean(values, -1, keepdims=True)
    centered = values - average
    inverse = lax.rsqrt(jnp.mean(centered * centered, -1, keepdims=True) + EPS)
    return centered * inverse, inverse


def norm_back(incoming, unit, inverse, gain_row):
    scaled = incoming * gain_row
    return inverse * (
        scaled
        - jnp.mean(scaled, -1, keepdims=True)
        - unit * jnp.mean(scaled * unit, -1, keepdims=True)
    )


def column_sum(values):
    return jnp.sum(values, 0, keepdims=True)


def spec_any():
    return pl.BlockSpec(memory_space=pl.ANY)


def spec_vmem():
    return pl.BlockSpec(memory_space=pltpu.VMEM)


def spec_smem():
    return pl.BlockSpec(memory_space=pltpu.SMEM)


def shaped(shape, kind=LOW):
    return jax.ShapeDtypeStruct(shape, kind)


def head_lanes(rows):
    return lax.broadcasted_iota(jnp.int32, (rows, PAIR), 1) < HEAD_DIM


def pick_head(values, lanes, head):
    zero = jnp.zeros_like(values)
    return jnp.where(lanes, values, zero) if head == 0 else jnp.where(lanes, zero, values)


def attend_tile(query, key_t, value, allowed, exp_ref, rows, width):
    lanes = head_lanes(query.shape[0])
    mixed, inverses = [], []
    for head in range(2):
        scores = dot(pick_head(query, lanes, head), key_t)
        scores = jnp.where(allowed, scores, NEG_FILL)
        top = jnp.max(scores, -1, keepdims=True)
        exponent = jnp.exp(scores - top)
        inverse = 1.0 / jnp.sum(exponent, -1, keepdims=True)
        low = exponent.astype(LOW)
        exp_ref[head, rows, 0:width] = low
        mixed.append(dot(low, value))
        inverses.append(inverse)
    inverse = jnp.where(lanes, inverses[0], inverses[1])
    return jnp.where(lanes, mixed[0], mixed[1]) * inverse, inverse


def self_allowed(offsets_ref, step, tile, width):
    places = lax.broadcasted_iota(jnp.int32, (tile, 1), 0) + step * tile
    begin = jnp.zeros((tile, 1), jnp.int32)
    for seg in range(1, 16):
        offset = offsets_ref[0, seg]
        begin = jnp.where(places >= offset, offset, begin)
    keys = lax.broadcasted_iota(jnp.int32, (tile, width), 1)
    return (keys <= places) & (keys >= begin)


def cross_allowed(ids, offsets_ref, pair_ref, step, tile):
    places = lax.broadcasted_iota(jnp.int32, (tile, 1), 0) + step * tile
    reads = jnp.zeros((tile, 1), jnp.int32) + pair_ref[0, 0]
    for seg in range(1, 16):
        reads = jnp.where(places >= offsets_ref[0, seg], pair_ref[0, seg], reads)
    return ids == reads


def aligned(index, unit):
    return pl.ds(pl.multiple_of(index * unit, unit), unit)


class Exchange:
    def __init__(self, send_sems, recv_sems, base):
        self.dp = lax.axis_index("dp")
        self.me = lax.axis_index("seq")
        self.send_sems, self.recv_sems, self.base = send_sems, recv_sems, base
        self.sent = []

    def copy(self, source, target, there, distance):
        return pltpu.make_async_remote_copy(
            src_ref=source,
            dst_ref=target,
            send_sem=self.send_sems.at[self.base + distance],
            recv_sem=self.recv_sems.at[self.base + distance],
            device_id=(self.dp, there),
            device_id_type=MESH,
        )

    def push(self, source, target, there, may_be_own):
        distance = lax.rem(there - self.me + SEQ, SEQ)
        if may_be_own:
            remote = there != self.me

            @pl.when(remote)
            def _():
                self.copy(source, target, there, distance).start()

        else:
            self.copy(source, target, there, distance).start()
        self.sent.append((source, target))

    def receive(self, place):
        for distance in range(1, SEQ):
            sender = lax.rem(self.me - distance + SEQ, SEQ)
            spot = place(sender)
            self.copy(spot, spot, sender, distance).wait_recv()

    def drain(self):
        source, target = self.sent[0]
        for distance in range(1, SEQ):
            there = lax.rem(self.me + distance, SEQ)
            self.copy(source, target, there, distance).wait_send()


def greet_row():
    dp = lax.axis_index("dp")
    me = lax.axis_index("seq")
    barrier = pltpu.get_barrier_semaphore()
    for distance in range(1, SEQ):
        pl.semaphore_signal(
            barrier, inc=1, device_id=(dp, lax.rem(me + distance, SEQ)), device_id_type=MESH
        )
    return barrier


class Gather:
    def __init__(self, block, spot, local_sem, send_sems, recv_sems, base):
        self.dp = lax.axis_index("dp")
        self.me = lax.axis_index("seq")
        self.y, self.xl = self.me // 2, lax.rem(self.me, 2)
        self.spot, self.send_sems, self.recv_sems, self.base = spot, send_sems, recv_sems, base
        self.own = pltpu.make_async_copy(block, spot(self.me), local_sem)
        self.block = block

    def part(self, y, xl):
        return self.spot(lax.rem(y + 8, 4) * 2 + xl)

    def copy(self, source, target, there, slot):
        return pltpu.make_async_remote_copy(
            src_ref=source,
            dst_ref=target,
            send_sem=self.send_sems.at[self.base + slot],
            recv_sem=self.recv_sems.at[self.base + slot],
            device_id=(self.dp, there),
            device_id_type=MESH,
        )

    def beside(self, step):
        return lax.rem(self.y + step + 4, 4) * 2 + self.xl

    def send(self, slot):
        y, xl = self.y, self.xl
        if slot == 0:
            return self.copy(self.block, self.part(y, xl), y * 2 + 1 - xl, 0)
        step = 1 if slot % 2 else -1
        if slot < 3:
            return self.copy(self.block, self.part(y, xl), self.beside(step), slot)
        spot = self.part(y, 1 - xl) if slot < 5 else self.part(y - step, xl if step == 1 else 1 - xl)
        return self.copy(spot, spot, self.beside(step), slot)

    def arrive(self, slot):
        y, xl = self.y, self.xl
        if slot == 0:
            spot = self.part(y, 1 - xl)
        else:
            step = 1 if slot % 2 else -1
            if slot < 5:
                spot = self.part(y - step, xl if slot < 3 else 1 - xl)
            else:
                spot = self.part(y + 2, xl if step == 1 else 1 - xl)
        self.copy(spot, spot, self.beside(1), slot).wait_recv()

    def first(self):
        self.own.start()
        for slot in range(3):
            self.send(slot).start()

    def second(self):
        self.arrive(0)
        for slot in (3, 4):
            self.send(slot).start()

    def third(self):
        self.arrive(1)
        self.send(5).start()
        self.arrive(4)
        self.send(6).start()

    def finish(self):
        for slot in (2, 3, 5, 6):
            self.arrive(slot)
        self.own.wait()
        for slot in range(7):
            self.send(slot).wait_send()


class Column:
    def __init__(self, block, spot, local_sem, send_sems, recv_sems, base):
        self.dp, self.me = lax.axis_index("dp"), lax.axis_index("seq")
        self.z = lax.rem(self.dp // 2, 4)
        self.block, self.spot, self.local_sem = block, spot, local_sem
        self.send_sems, self.recv_sems, self.base = send_sems, recv_sems, base

    def at(self, step):
        return self.spot(lax.rem(self.z + step + 4, 4))

    def copy(self, source, target, step, slot):
        there = self.dp + 2 * (lax.rem(self.z + step + 4, 4) - self.z)
        return pltpu.make_async_remote_copy(
            src_ref=source,
            dst_ref=target,
            send_sem=self.send_sems.at[self.base + slot],
            recv_sem=self.recv_sems.at[self.base + slot],
            device_id=(there, self.me),
            device_id_type=MESH,
        )

    def own(self):
        return pltpu.make_async_copy(self.block, self.at(0), self.local_sem)

    def half(self, step, slot):
        return self.at(step).at[pl.ds(0 if slot == 2 else TOK // 2, TOK // 2), :]

    def first(self):
        if self.local_sem is not None:
            self.own().start()
        self.copy(self.block, self.at(0), 1, 0).start()
        self.copy(self.block, self.at(0), -1, 1).start()

    def second(self):
        for slot, step in ((0, 1), (1, -1)):
            self.copy(self.block, self.at(-step), step, slot).wait_recv()
            piece = self.half(-step, slot + 2)
            self.copy(piece, piece, step, slot + 2).start()

    def near(self):
        for slot, step in ((0, 1), (1, -1)):
            self.copy(self.block, self.at(-step), step, slot).wait_recv()
            self.copy(self.block, self.at(0), step, slot).wait_send()
        self.own().wait()

    def sent_near(self):
        for slot, step in ((0, 1), (1, -1)):
            self.copy(self.block, self.at(0), step, slot).wait_send()

    def forward(self):
        for slot, step in ((0, 1), (1, -1)):
            piece = self.half(-step, slot + 2)
            self.copy(piece, piece, step, slot + 2).start()

    def far(self):
        for slot, step in ((0, 1), (1, -1)):
            piece = self.half(2, slot + 2)
            self.copy(piece, piece, step, slot + 2).wait_recv()
            piece = self.half(-step, slot + 2)
            self.copy(piece, piece, step, slot + 2).wait_send()

    def finish(self):
        self.far()
        for slot, step in ((0, 1), (1, -1)):
            self.copy(self.block, self.at(0), step, slot).wait_send()
        if self.local_sem is not None:
            self.own().wait()


def front_kernel(
    tok_ref, mem_ref, cot_ref, gain_ref, bias_ref, ids_ref, offsets_ref, pair_ref,
    qkv_hbm, ckv_hbm, out_hbm, query_hbm,
    x1_ref, n2_ref, o1_ref, o2_ref, heads_ref, memh_ref, cqh_ref, mix1_ref, mix2_ref,
    inv1_ref, inv2_ref, n1_ref, exp1_hbm, exp2_hbm, cot_all, mem_all, n2_all, o1_all,
    qkv_w, ckv_w, out_w, query_w, give_heads, give_mem, cq_ref, exp1_ref, exp2_ref,
    load_sems, keep_sems, exp_sems, send_sems, recv_sems,
):
    me = lax.axis_index("seq")
    y, xl = me // 2, lax.rem(me, 2)
    dp = lax.axis_index("dp")
    barrier = greet_row()
    for step in (1, 2, 3):
        z = lax.rem(dp // 2, 4)
        there = dp + 2 * (lax.rem(z + step, 4) - z)
        pl.semaphore_signal(barrier, inc=1, device_id=(there, me), device_id_type=MESH)
    order = [lax.rem(y + step, 4) for step in (1, 2, 3, 0)]
    loads = {}
    for step in range(4):
        for part in range(3):
            cols = pl.ds(pl.multiple_of(part * WIDTH + order[step] * 256, 256), 256)
            loads["qkv", step, part] = pltpu.make_async_copy(
                qkv_hbm.at[:, cols], qkv_w.at[:, cols], load_sems.at[step * 3 + part]
            )
    for step in range(4):
        for part in range(2):
            cols = pl.ds(pl.multiple_of(part * WIDTH + order[step] * 256, 256), 256)
            loads["ckv", step, part] = pltpu.make_async_copy(
                ckv_hbm.at[:, cols], ckv_w.at[:, cols], load_sems.at[12 + step * 2 + part]
            )
    loads["out"] = pltpu.make_async_copy(out_hbm, out_w, load_sems.at[20])
    loads["query"] = pltpu.make_async_copy(query_hbm, query_w, load_sems.at[21])
    for name, one in loads.items():
        if name[0] == "qkv":
            one.start()

    give_qkv, give_kv, back1, give_q, back2 = (
        Exchange(send_sems, recv_sems, 8 * index) for index in range(5)
    )
    own_rows = aligned(me, TOK)
    columns = [
        Column(
            block, lambda at, whole=whole: whole.at[at], keep_sems.at[7 + index],
            send_sems, recv_sems, 40 + 4 * index,
        )
        for index, (block, whole) in enumerate(
            ((cot_ref, cot_all), (mem_ref, mem_all), (o1_ref, o1_all), (n2_ref, n2_all))
        )
    ]

    unit, _ = norm_unit(tok_ref[...].astype(F32))
    n1 = (unit * gain_ref[0:1, :] + bias_ref[0:1, :]).astype(LOW)
    n1_ref[...] = n1
    mem = mem_ref[...]
    for kind, count, source, give, heads, exchange in (
        ("qkv", 3, n1, give_heads, heads_ref, give_qkv),
        ("ckv", 2, mem, give_mem, memh_ref, give_kv),
    ):
        for step in range(4):
            at = order[step]
            own = aligned(at, 256)
            for part in range(count):
                loads[kind, step, part].wait()
                cols = pl.ds(pl.multiple_of(part * WIDTH + at * 256, 256), 256)
                if kind == "qkv":
                    value = dot(source, qkv_w[:, cols])
                    if part == 0:
                        value = (value + bias_ref[3:4, own]) * SCALE
                    elif part == 2:
                        value = value + bias_ref[4:5, own]
                else:
                    value = dot(source, ckv_w[:, cols])
                    if part == 1:
                        value = value + bias_ref[7:8, own]
                low = value.astype(LOW)
                give[2 * at, :, part * PAIR : part * PAIR + PAIR] = low[:, :PAIR]
                give[2 * at + 1, :, part * PAIR : part * PAIR + PAIR] = low[:, PAIR:]
            if kind == "qkv" and step == 0:
                for name, one in loads.items():
                    if name[0] != "qkv":
                        one.start()
                pl.semaphore_wait(barrier, SEQ - 1 + 3)
                columns[0].first()
                columns[1].first()
            there = heads.at[own_rows, :]
            if step < 3:
                exchange.push(give.at[2 * at], there, 2 * at, False)
                exchange.push(give.at[2 * at + 1], there, 2 * at + 1, False)
            else:
                partner = 2 * y + 1 - xl
                exchange.push(give.at[partner], there, partner, False)
                keep = pltpu.make_async_copy(
                    give.at[me], there, keep_sems.at[2 if kind == "qkv" else 3]
                )
                keep.start()
                loads[kind] = keep

    def attended(allowed_of, query_of, key_t, value_ref, value_at, mix_ref, inv_ref, exp_ref,
                 exp_hbm, exp_base, causal, back, target_ref, keep_sem):
        tile = 256
        for step in range(ROW // tile):
            rows = slice(step * tile, step * tile + tile)
            width = (step + 1) * tile if causal else ROW
            mixture, inverse = attend_tile(
                query_of(rows), key_t[:, 0:width], value_ref[0:width, value_at], allowed_of(step, width),
                exp_ref, rows, width,
            )
            mix_ref[rows, :] = mixture.astype(LOW)
            inv_ref[rows, :] = inverse
            for half in range(2):
                there = 2 * step + half
                back.push(
                    mix_ref.at[there * TOK : there * TOK + TOK, :],
                    target_ref.at[:, aligned(me, PAIR)], there, True,
                )
            for head in range(2):
                spot = (head, rows, slice(0, width))
                pltpu.make_async_copy(
                    exp_ref.at[spot], exp_hbm.at[spot], exp_sems.at[exp_base + step * 2 + head]
                ).start()
        keep = pltpu.make_async_copy(
            mix_ref.at[own_rows, :], target_ref.at[:, aligned(me, PAIR)], keep_sem
        )
        keep.start()
        return keep

    loads["qkv"].wait()
    give_qkv.receive(lambda sender: heads_ref.at[aligned(sender, TOK), :])
    key_t = heads_ref[:, PAIR : 2 * PAIR].T
    keep1 = attended(
        lambda step, width: self_allowed(offsets_ref, step, 256, width),
        lambda rows: heads_ref[rows, 0:PAIR], key_t, heads_ref, slice(2 * PAIR, 3 * PAIR),
        mix1_ref, inv1_ref, exp1_ref, exp1_hbm, 0, True, back1, o1_ref, keep_sems.at[4],
    )
    columns[0].second()
    columns[1].second()
    keep1.wait()
    loads["out"].wait()
    back1.receive(lambda sender: o1_ref.at[:, aligned(sender, PAIR)])
    columns[2].first()
    x1 = tok_ref[...].astype(F32) + dot(o1_ref[...], out_w[...]) + bias_ref[5:6, :]
    x1_ref[...] = x1
    unit, _ = norm_unit(x1)
    n2 = (unit * gain_ref[1:2, :] + bias_ref[1:2, :]).astype(LOW)
    n2_ref[...] = n2
    columns[3].first()
    loads["query"].wait()
    for step in range(4):
        at = order[step]
        own = aligned(at, 256)
        cq_ref[:, own] = ((dot(n2, query_w[:, own]) + bias_ref[6:7, own]) * SCALE).astype(LOW)
        for half in range(2):
            there = 2 * at + half if step < 3 else 2 * y + 1 - xl
            if step == 3 and half == 1:
                continue
            give_q.push(cq_ref.at[:, aligned(there, PAIR)], cqh_ref.at[own_rows, :], there, False)
    keep = pltpu.make_async_copy(cq_ref.at[:, aligned(me, PAIR)], cqh_ref.at[own_rows, :], keep_sems.at[5])
    keep.start()
    loads["ckv"].wait()
    give_kv.receive(lambda sender: memh_ref.at[aligned(sender, TOK), :])
    key_t = memh_ref[:, 0:PAIR].T
    keep.wait()
    give_q.receive(lambda sender: cqh_ref.at[aligned(sender, TOK), :])
    ids = ids_ref[...]
    keep2 = attended(
        lambda step, width: cross_allowed(ids, offsets_ref, pair_ref, step, 256),
        lambda rows: cqh_ref[rows, :], key_t, memh_ref, slice(PAIR, 2 * PAIR),
        mix2_ref, inv2_ref, exp2_ref, exp2_hbm, 8, False, back2, o2_ref, keep_sems.at[6],
    )
    keep2.wait()
    back2.receive(lambda sender: o2_ref.at[:, aligned(sender, PAIR)])
    for step in range(4):
        rows = slice(step * 256, step * 256 + 256)
        for head in range(2):
            spot = (head, rows, slice(0, step * 256 + 256))
            pltpu.make_async_copy(
                exp1_ref.at[spot], exp1_hbm.at[spot], exp_sems.at[step * 2 + head]
            ).wait()
            spot = (head, rows, slice(0, ROW))
            pltpu.make_async_copy(
                exp2_ref.at[spot], exp2_hbm.at[spot], exp_sems.at[8 + step * 2 + head]
            ).wait()
    for exchange in (give_qkv, give_kv, back1, give_q, back2):
        exchange.drain()
    for column in columns[:2]:
        column.finish()
    for column in columns[2:]:
        column.near()


def front_call(operands):
    dma = pltpu.SemaphoreType.DMA
    vmem = pltpu.VMEM
    heads = shaped((ROW, PAIR))
    token = shaped((TOK, WIDTH))
    inverse = shaped((ROW, PAIR), F32)
    exps = shaped((2, ROW, ROW))
    four = shaped((4, TOK, WIDTH))
    return pl.pallas_call(
        front_kernel,
        out_shape=(
            shaped((TOK, WIDTH), F32), token, token, token, shaped((ROW, 3 * PAIR)),
            shaped((ROW, 2 * PAIR)), heads, heads, heads, inverse, inverse, token,
            exps, exps, four, four, four, four,
        ),
        in_specs=[spec_vmem()] * 6 + [spec_smem()] * 2 + [spec_any()] * 4,
        out_specs=(spec_vmem(),) * 12 + (spec_any(),) * 6,
        scratch_shapes=[
            vmem((WIDTH, 3 * WIDTH), LOW), vmem((WIDTH, 2 * WIDTH), LOW), vmem((WIDTH, WIDTH), LOW),
            vmem((WIDTH, WIDTH), LOW), vmem((SEQ, TOK, 3 * PAIR), LOW), vmem((SEQ, TOK, 2 * PAIR), LOW),
            vmem((TOK, WIDTH), LOW), vmem((2, ROW, ROW), LOW), vmem((2, ROW, ROW), LOW),
            dma((22,)), dma((11,)), dma((16,)), dma((56,)), dma((56,)),
        ],
        compiler_params=pltpu.CompilerParams(
            collective_id=2, has_side_effects=True, vmem_limit_bytes=56 * MIB
        ),
        cost_estimate=pl.CostEstimate(
            flops=2 * TOK * WIDTH * 7 * WIDTH, bytes_accessed=60 * MIB, transcendentals=0
        ),
        name="front",
    )(*operands)


LANES = 256


def wrap(index):
    return lax.rem(index + 8, 4)


def device_of(core, x, y, z):
    return ((x // 2) * 8 + z * 2 + core, y * 2 + lax.rem(x, 2))


class Place:
    def __init__(self):
        self.dp = lax.axis_index("dp")
        self.seq = lax.axis_index("seq")
        self.core = lax.rem(self.dp, 2)
        self.y, self.xl = self.seq // 2, lax.rem(self.seq, 2)
        self.at = {
            "x": (self.dp // 8) * 2 + self.xl,
            "y": self.y,
            "z": lax.rem(self.dp // 2, 4),
        }
        self.z = self.at["z"]
        self.other = (self.dp + 1 - 2 * self.core, self.seq)
        self.rank = lax.rem(self.dp, 8)

    def member(self, distance):
        rank = lax.rem(self.rank + distance + 8, 8)
        return (self.dp - self.rank + rank, self.seq), rank

    def neighbour(self, axis, step):
        at = dict(self.at)
        at[axis] = wrap(at[axis] + step)
        return device_of(self.core, **at)


class Sum:
    def __init__(self, place, grads, lands, flows, send_sems, recv_sems, base):
        self.place, self.grads, self.lands, self.flows = place, grads, lands, flows
        self.send_sems, self.recv_sems, self.base = send_sems, recv_sems, base
        self.open_sends = []

    def view(self, order, stage, block, first, rows):
        index = {"x": slice(None), "y": slice(None)}
        for done in range(stage):
            index[order[done]] = self.place.at[order[done]]
        index[order[stage]] = block
        return (index["x"], index["y"], slice(first, first + rows), slice(None))

    def land(self, stage, slot, first, rows):
        return (slot,) + (slice(None),) * (1 - stage) + (slice(first, first + rows), slice(None))

    def spans(self, flow):
        order, first, low, high = self.flows[flow]
        return order, (first, low), (first + low, high)

    def copy(self, stage, flow, kind):
        order, low, high = self.spans(flow)
        axis = order[stage]
        step = (2, 2, 1, -1, 1, -1)[kind]
        way = (1, -1, 1, -1, 1, -1)[kind]
        first, rows = (low, high, high, low, low, high)[kind]
        slot = (0, 0, 1, 1, 2, 2)[kind]
        at = self.base + (stage * len(self.flows) + flow) * 6 + kind
        return pltpu.make_async_remote_copy(
            src_ref=self.grads.at[
                self.view(order, stage, wrap(self.place.at[axis] + step), first, rows)
            ],
            dst_ref=self.lands[stage].at[self.land(stage, slot, first, rows)],
            send_sem=self.send_sems.at[at],
            recv_sem=self.recv_sems.at[at],
            device_id=self.place.neighbour(axis, way),
            device_id_type=MESH,
        )

    def straight(self, stage, flow, distance):
        order, (first, low), (_, high) = self.spans(flow)
        axis, rows = order[stage], low + high
        at = self.base + (stage * len(self.flows) + flow) * 6 + distance
        return pltpu.make_async_remote_copy(
            src_ref=self.grads.at[
                self.view(order, stage, wrap(self.place.at[axis] + distance), first, rows)
            ],
            dst_ref=self.lands[stage].at[self.land(stage, distance - 1, first, rows)],
            send_sem=self.send_sems.at[at],
            recv_sem=self.recv_sems.at[at],
            device_id=self.place.neighbour(axis, distance),
            device_id_type=MESH,
        )

    def add(self, stage, flow, step, span, slots):
        order, _, _ = self.spans(flow)
        at = self.view(order, stage, wrap(self.place.at[order[stage]] + step), *span)
        total = self.grads[at].astype(F32)
        for slot in slots:
            total = total + self.lands[stage][self.land(stage, slot, *span)].astype(F32)
        self.grads[at] = total.astype(LOW)

    def start(self, copy):
        copy.start()
        self.open_sends.append(copy)

    def run(self):
        flows = range(len(self.flows))
        for kind in range(4):
            for flow in flows:
                self.start(self.copy(0, flow, kind))
        yield
        for flow in flows:
            _, low, high = self.spans(flow)
            self.copy(0, flow, 0).wait_recv()
            self.add(0, flow, 1, low, (0,))
            self.start(self.copy(0, flow, 4))
            self.copy(0, flow, 1).wait_recv()
            self.add(0, flow, -1, high, (0,))
            self.start(self.copy(0, flow, 5))
        yield
        for flow in flows:
            _, low, high = self.spans(flow)
            for kind in (2, 3, 4, 5):
                self.copy(0, flow, kind).wait_recv()
            self.add(0, flow, 0, low, (1, 2))
            self.add(0, flow, 0, high, (1, 2))
            for distance in (1, 2, 3):
                self.start(self.straight(1, flow, distance))
        yield
        for flow in flows:
            _, low, high = self.spans(flow)
            for distance in (1, 2, 3):
                self.straight(1, flow, distance).wait_recv()
            self.add(1, flow, 0, (low[0], low[1] + high[1]), (0, 1, 2))
        yield

    def run_straight(self):
        flows = range(len(self.flows))
        for stage in range(2):
            for flow in flows:
                for distance in (1, 2, 3):
                    self.start(self.straight(stage, flow, distance))
            yield
            for flow in flows:
                _, low, high = self.spans(flow)
                for distance in (1, 2, 3):
                    self.straight(stage, flow, distance).wait_recv()
                self.add(stage, flow, 0, (low[0], low[1] + high[1]), (0, 1, 2))
        yield

    def drain(self):
        for copy in self.open_sends:
            copy.wait_send()
        self.open_sends = []


FF_CHUNK = 512
HALF_CHUNKS = FF // FF_CHUNK // 2
FLOWS_F = (("xy", 0, 64, 64), ("yx", 128, 64, 64))
FLOWS_C = (("xy", 0, 32, 32), ("yx", 64, 32, 32))


class Eight:
    def __init__(self, place, send_sems, recv_sems, base):
        self.place, self.send_sems, self.recv_sems = place, send_sems, recv_sems
        self.base, self.last = base, None

    def copy(self, source, target, distance):
        device, _ = self.place.member(distance)
        return pltpu.make_async_remote_copy(
            src_ref=source,
            dst_ref=target,
            send_sem=self.send_sems.at[self.base + distance],
            recv_sem=self.recv_sems.at[self.base + distance],
            device_id=device,
            device_id_type=MESH,
        )

    def push(self, source_of, target):
        for distance in range(1, 8):
            _, rank = self.place.member(distance)
            self.last = (source_of(rank), target)
            self.copy(source_of(rank), target, distance).start()

    def receive(self, place_of):
        for distance in range(1, 8):
            _, rank = self.place.member(-distance)
            spot = place_of(rank)
            self.copy(spot, spot, distance).wait_recv()

    def drain(self):
        for distance in range(1, 8):
            self.copy(*self.last, distance).wait_send()


def back_kernel(
    gain_ref, bias_ref, ebias_ref,
    o2_hbm, x1_hbm, cot_hbm, tok_hbm, n1_hbm, cot4_hbm, mem4_hbm, n24_hbm, o14_hbm,
    heads_hbm, memh_hbm, cqh_hbm, mix1_hbm, mix2_hbm, inv1_hbm, inv2_hbm, exp1_hbm, exp2_hbm,
    qkv_hbm, ckv_hbm, out_hbm, query_hbm, cross_hbm, expand_hbm, reduce_hbm,
    output_ref, gtok_ref, gmem_ref, all_f, all_c, all_q, all_v,
    n1_all, ring_e, ring_r, cross_w, exp_ref, x1_ref, cot_ref, tok_ref,
    heads_ref, memh_ref, cqh_ref, mix1_ref, mix2_ref, inv1_ref, inv2_ref,
    a_n3, a_cot, a_o2, a_n2, a_o1, a_mem, act_in, dfe_in, act_out, dfe_out,
    b_dc, b_e2, b_da, b_kv,
    dc_ref, da_ref, acc_ref, dn_ref, expand_sums, vec_ref,
    do2_ref, do1_ref, do2h_ref, do1h_ref, sums_ref, e2_ref, dkv_ref, e1_ref, dkt_ref, dvt_ref,
    grads_f, land_f1, land_f2, grads_c, land_c1, land_c2,
    piece_f, piece_c, weight_ref, weight_in, weight_sum, piece_q, vec_out, vec_in, piece_v,
    load_sems, ring_sems, keep_sems, pair_send, pair_recv, send_sems, recv_sems,
    dp_send, dp_recv, sum_send, sum_recv, eight_send, eight_recv, column_send, column_recv,
):
    place = Place()
    core, y, xl, me, dp = place.core, place.y, place.xl, place.seq, place.dp
    partner = 2 * y + 1 - xl
    own_rows = aligned(me, TOK)
    order = [lax.rem(y + step, 4) for step in (1, 2, 3, 0)]

    barrier = greet_row()
    for distance in range(1, DP):
        pl.semaphore_signal(
            barrier, inc=1, device_id=(lax.rem(dp + distance, DP), me), device_id_type=MESH
        )
    outer = place.neighbour("x", 2 * xl - 1)
    pl.semaphore_signal(barrier, inc=1, device_id=outer, device_id_type=MESH)

    def load(source, target, sem):
        copy = pltpu.make_async_copy(source, target, load_sems.at[sem])
        copy.start()
        return copy

    z, rank = place.z, place.rank
    rank_rows = aligned(rank, TOK)

    def chunk_of(step):
        return lax.rem(rank + 1 + step, 8)

    def ring_copies(step, slot):
        copies = []
        for block in range(2):
            span = aligned(chunk_of(step) + 8 * block, 256)
            to = pl.ds(pl.multiple_of(slot * FF_CHUNK + block * 256, 256), 256)
            at = slot * 4 + block * 2
            copies += [
                pltpu.make_async_copy(expand_hbm.at[:, span], ring_e.at[:, to], ring_sems.at[at]),
                pltpu.make_async_copy(
                    reduce_hbm.at[span, :], ring_r.at[to, :], ring_sems.at[at + 1]
                ),
            ]
        return copies

    loads = [
        load(o2_hbm, a_o2.at[z, core], 0), load(cross_hbm, cross_w, 1), load(x1_hbm, x1_ref, 2),
        load(cot_hbm, cot_ref, 3)
    ]
    gather = Gather(
        n1_hbm, lambda at: n1_all.at[aligned(at, TOK), :], keep_sems.at[0], send_sems, recv_sems, 64
    )
    gather_f = Gather(
        piece_f, lambda at: all_f.at[at], keep_sems.at[13], send_sems, recv_sems, 79
    )
    col_n3, col_o2, col_n2, col_o1 = (
        Column(
            block, lambda at, whole=whole: whole.at[at, core], None,
            column_send, column_recv, 4 * index,
        )
        for index, (block, whole) in enumerate(
            (
                (a_n3.at[z, core], a_n3), (o2_hbm, a_o2), (a_n2.at[z, core], a_n2),
                (a_o1.at[z, core], a_o1),
            )
        )
    )
    to_core = []

    def both_cores(whole):
        slot = len(to_core)
        copy = pltpu.make_async_remote_copy(
            src_ref=whole.at[:, core],
            dst_ref=whole.at[:, core],
            send_sem=pair_send.at[slot],
            recv_sem=pair_recv.at[slot],
            device_id=place.other,
            device_id_type=MESH,
        )
        copy.start()
        arrival = pltpu.make_async_remote_copy(
            src_ref=whole.at[:, 1 - core],
            dst_ref=whole.at[:, 1 - core],
            send_sem=pair_send.at[slot],
            recv_sem=pair_recv.at[slot],
            device_id=place.other,
            device_id_type=MESH,
        )
        to_core.append((copy, arrival))

    blocks_to_core = []

    def block_to_core(whole, step):
        slot = 7 + len(blocks_to_core)
        at = lax.rem(z + step + 4, 4)

        def copy(half):
            return pltpu.make_async_remote_copy(
                src_ref=whole.at[at, half],
                dst_ref=whole.at[at, half],
                send_sem=pair_send.at[slot],
                recv_sem=pair_recv.at[slot],
                device_id=place.other,
                device_id_type=MESH,
            )

        copy(core).start()
        blocks_to_core.append((copy(core), copy(1 - core)))

    give_act, give_dfe, give_dc, give_be2, give_kv, give_da, join_f, join_c = (
        Eight(place, eight_send, eight_recv, 8 * index) for index in range(8)
    )

    for one in loads[:3]:
        one.wait()
    for step in range(4):
        for one in ring_copies(step, step):
            one.start()
    x2 = x1_ref[...] + dot(a_o2[z, core], cross_w[...]) + bias_ref[8:9, :]
    unit3, inverse3 = norm_unit(x2)
    a_n3[z, core] = (unit3 * gain_ref[2:3, :] + bias_ref[2:3, :]).astype(LOW)
    acc_ref[...] = x2 + bias_ref[9:10, :]
    dn_ref[...] = jnp.zeros_like(dn_ref)
    loads[3].wait()
    pl.semaphore_wait(barrier, SEQ - 1 + DP - 1 + 1)
    gather.first()
    col_n3.first()
    root = math.sqrt(2.0 / math.pi)

    def feed(step, slot, own):
        for one in ring_copies(step, slot):
            one.wait()
        chunk = chunk_of(step)
        span = aligned(slot, FF_CHUNK)
        offset = jnp.concatenate(
            [ebias_ref[:, aligned(chunk + 8 * block, 256)] for block in range(2)], 1
        )
        hidden = dot(a_n3[z, core], ring_e[:, span]) + offset
        square = hidden * hidden
        curve = jnp.tanh(root * hidden * (1.0 + 0.044715 * square))
        share = 0.5 * (1.0 + curve)
        act = (hidden * share).astype(LOW)
        slope = share + 0.5 * hidden * (1.0 - curve * curve) * (
            root * (1.0 + 3.0 * 0.044715 * square)
        )
        acc_ref[...] += dot(act, ring_r[span, :])
        grad_act = dot_nt(cot_ref[...], ring_r[span, :])
        grad_hidden = (slope * grad_act).astype(LOW)
        if own:
            act_in[rank_rows, :] = act
            dfe_in[rank_rows, :] = grad_hidden
        else:
            act_out[step] = act
            dfe_out[step] = grad_hidden
            give_act.copy(act_out.at[step], act_in.at[rank_rows, :], step + 1).start()
            give_dfe.copy(dfe_out.at[step], dfe_in.at[rank_rows, :], step + 1).start()
        expand_sums[chunk] = column_sum(grad_hidden.astype(F32))
        dn_ref[...] += dot_nt(grad_hidden, ring_e[:, span])

    gathered = [
        (source.at[at], whole.at[at, core])
        for source, whole, steps in (
            (cot4_hbm, a_cot, (0, 1, 2, 3)), (mem4_hbm, a_mem, (0, 1, 2, 3)),
            (n24_hbm, a_n2, (-1, 0, 1)), (o14_hbm, a_o1, (-1, 0, 1)),
        )
        for at in [lax.rem(z + step + 4, 4) for step in steps]
    ]
    gathered = [
        pltpu.make_async_copy(source, target, load_sems.at[24 + index])
        for index, (source, target) in enumerate(gathered)
    ]

    def feed_step(step, carry):
        feed(step, lax.rem(step, 4), False)

        @pl.when(step < 4)
        def _():
            for one in ring_copies(step + 4, step):
                one.start()

        @pl.when(step == 2)
        def _():
            gather.second()

        @pl.when(step == 4)
        def _():
            col_n3.second()

        return carry

    lax.fori_loop(0, 7, feed_step, 0)
    feed(7, 3, True)
    give_act.last = (act_out.at[0], act_in.at[rank_rows, :])
    give_dfe.last = (dfe_out.at[0], dfe_in.at[rank_rows, :])
    col_o2.first()
    for one in gathered:
        one.start()
    kept = [
        load(memh_hbm, memh_ref, 9), load(cqh_hbm, cqh_ref, 10), load(mix2_hbm, mix2_ref, 11),
        load(inv2_hbm, inv2_ref, 12), load(exp2_hbm, exp_ref, 13),
    ]
    later = [
        load(query_hbm, ring_r.at[1024:2048, :], 14), load(out_hbm, ring_r.at[0:1024, :], 15),
        load(ckv_hbm, ring_e, 16),
    ]
    kept1 = [
        load(heads_hbm, heads_ref, 17), load(mix1_hbm, mix1_ref, 18), load(inv1_hbm, inv1_ref, 19),
        load(tok_hbm, tok_ref, 20),
    ]
    output_ref[...] = acc_ref[...].astype(LOW)
    dn3 = dn_ref[...]
    grad = cot_ref[...].astype(F32)
    dx2 = grad + norm_back(dn3, unit3, inverse3, gain_ref[2:3, :])
    acc_ref[...] = dx2
    dc_ref[...] = dx2.astype(LOW)

    give_do2, give_e2, give_k2, give_v2, give_do1, give_q1, give_k1, give_v1 = (
        Exchange(send_sems, recv_sems, 8 * index) for index in range(8)
    )

    def push_heads(exchange, low_ref, weight_of, values, target, keep_slot):
        for step in range(4):
            at = order[step]
            low_ref[:, aligned(at, 256)] = dot_nt(values, weight_of(aligned(at, 256))).astype(LOW)
            if step < 3:
                for half in range(2):
                    there = 2 * at + half
                    exchange.push(
                        low_ref.at[:, aligned(there, PAIR)], target.at[own_rows, :], there, False
                    )
            else:
                exchange.push(
                    low_ref.at[:, aligned(partner, PAIR)], target.at[own_rows, :], partner, False
                )
        keep = pltpu.make_async_copy(
            low_ref.at[:, aligned(me, PAIR)], target.at[own_rows, :], keep_sems.at[keep_slot]
        )
        keep.start()
        return keep

    keep_do2 = push_heads(
        give_do2, do2_ref, lambda rows: cross_w[rows, :], dc_ref[...], do2h_ref, 1
    )

    def share(exchange, source, target, width):
        exchange.push(lambda to: source.at[:, aligned(to, width)], target.at[rank_rows, :])
        target[rank_rows, :] = source[:, aligned(rank, width)]

    share(give_dc, dc_ref, b_dc, PAIR)
    vec_ref[2:3, :] = column_sum(dn3 * unit3)
    vec_ref[5:6, :] = column_sum(dn3)
    vec_ref[11:12, :] = column_sum(dc_ref[...].astype(F32))
    vec_ref[12:13, :] = column_sum(grad)

    def left_of(whole, group):
        return whole[:, :, :, aligned(group, 128)].reshape(ROW, 128)

    def rows_of(group, block):
        to = lax.rem(group, 4) * 2 + block
        return pl.ds(pl.multiple_of(to * 16, 16), 16)

    def fill_f(group, carry):
        result = dot_tn(left_of(a_n3, group), dfe_in[...]).astype(LOW)
        for block in range(2):
            for yy in range(4):
                at = (block * 4 + yy) * 16
                for col in range(2):
                    grads_f[(group // 4) * 2 + col, yy, rows_of(group, block), :] = result[
                        at : at + 16, col * LANES : col * LANES + LANES
                    ]
        return carry

    def fill_reduce():
        for xh in range(2):
            result = dot_tn(
                act_in[:, xh * 256 : xh * 256 + 256], a_cot[...].reshape(ROW, WIDTH)
            ).astype(LOW)
            for yy in range(4):
                for col in range(2):
                    for sub in range(2):
                        at = (col * 2 + sub) * LANES
                        grads_f[xh * 2 + col, yy, 128 + sub * 64 : 192 + sub * 64, :] = result[
                            yy * 64 : yy * 64 + 64, at : at + LANES
                        ]

    def fill_c():
        parts = ((a_n2, b_e2, 0, 0, PAIR), (a_o1, b_da, 0, PAIR, PAIR), (a_o2, b_dc, 0, 2 * PAIR, PAIR),
                 (a_mem, b_kv, 1, 0, 256))
        for whole, right, x_at, lane, width in parts:
            result = dot_tn(right[...], whole[...].reshape(ROW, WIDTH)).T.astype(LOW)
            for xh in range(2):
                for to in range(8):
                    for yy in range(4):
                        at = xh * 512 + to * 64 + yy * 16
                        grads_c[
                            xh * 2 + x_at, yy, to * 16 : to * 16 + 16, lane : lane + width
                        ] = result[at : at + 16, :]
        for xh in range(2):
            grads_c[xh * 2 + 1, :, :, 256:384] = jnp.zeros((4, 128, PAIR), LOW)

    sum_f = Sum(place, grads_f, (land_f1, land_f2), FLOWS_F, sum_send, sum_recv, 0)
    sum_c = Sum(place, grads_c, (land_c1, land_c2), FLOWS_C, sum_send, sum_recv, 24)
    run_f, run_c = sum_f.run(), sum_c.run_straight()

    def attend_back(query, key_rows, value_rows, grad_ref, mix_ref, inv_ref, causal, after_tile):
        tile = 256
        scaled = (grad_ref[...].astype(F32) * inv_ref[...]).astype(LOW)
        lanes = head_lanes(ROW)
        product = scaled.astype(F32) * mix_ref[...].astype(F32)
        inner = [jnp.sum(pick_head(product, lanes, head), -1, keepdims=True) for head in range(2)]
        value_t = value_rows.T
        query_t = query.T
        scaled_t = scaled.T
        dkt_ref[...] = jnp.zeros_like(dkt_ref)
        dvt_ref[...] = jnp.zeros_like(dvt_ref)
        tile_lanes = head_lanes(tile)
        steps = range(ROW // tile)
        for step in reversed(steps) if causal else steps:
            rows = slice(step * tile, step * tile + tile)
            width = (step + 1) * tile if causal else ROW
            parts = []
            for head in range(2):
                own = slice(head * HEAD_DIM, head * HEAD_DIM + HEAD_DIM)
                exponent = exp_ref[head, rows, 0:width]
                grad_p = dot(pick_head(scaled[rows, :], tile_lanes, head), value_t[:, 0:width])
                grad_s = (exponent.astype(F32) * (grad_p - inner[head][rows, :])).astype(LOW)
                parts.append(dot(grad_s, key_rows[0:width, :]))
                dkt_ref[own, 0:width] += dot(query_t[own, rows], grad_s)
                dvt_ref[own, 0:width] += dot(scaled_t[own, rows], exponent)
            grad_q = jnp.where(tile_lanes, parts[0], parts[1]).astype(LOW) * SCALE
            sums_ref[rows, 0:PAIR] = grad_q.astype(LOW)
            after_tile(step, rows)

    def send_part(exchange, part, there, target, column):
        exchange.push(
            sums_ref.at[there * TOK : there * TOK + TOK, part * PAIR : part * PAIR + PAIR],
            target.at[:, pl.ds(pl.multiple_of(column + me * PAIR, PAIR), PAIR)], there, True,
        )

    def keep_part(part, target, column, slot):
        copy = pltpu.make_async_copy(
            sums_ref.at[own_rows, part * PAIR : part * PAIR + PAIR],
            target.at[:, pl.ds(pl.multiple_of(column + me * PAIR, PAIR), PAIR)],
            keep_sems.at[slot],
        )
        copy.start()
        return copy

    def from_peers(target, column):
        return lambda sender: target.at[
            :, pl.ds(pl.multiple_of(column + sender * PAIR, PAIR), PAIR)
        ]

    def join(exchange, grads, piece, keep_slot, rest):
        block = grads.at[place.at["x"], place.at["y"]]
        mine = pl.ds(pl.multiple_of(rank * 16, 16), 16)
        exchange.push(
            lambda to: block.at[pl.ds(pl.multiple_of(to * 16, 16), 16), :], piece.at[mine, :]
        )
        keeps = [
            pltpu.make_async_copy(block.at[mine, :], piece.at[mine, :], keep_sems.at[keep_slot])
        ]
        if rest:
            keeps.append(
                pltpu.make_async_copy(
                    block.at[pl.ds(128, 128), :], piece.at[pl.ds(128, 128), :],
                    keep_sems.at[keep_slot + 1],
                )
            )
        for one in keeps:
            one.start()
        return keeps

    def joined(exchange, piece, keeps):
        for one in keeps:
            one.wait()
        exchange.receive(lambda to: piece.at[pl.ds(pl.multiple_of(to * 16, 16), 16), :])

    spreads = []

    def spread(piece, whole, base, slot):
        exchange = Exchange(send_sems, recv_sems, base)
        for distance in range(1, SEQ):
            exchange.push(piece, whole.at[me], lax.rem(me + distance, SEQ), False)
        keep = pltpu.make_async_copy(piece, whole.at[me], keep_sems.at[slot])
        keep.start()
        spreads.append((exchange, keep, whole))

    for one in kept:
        one.wait()
    keep_do2.wait()
    give_do2.receive(lambda sender: do2h_ref.at[aligned(sender, TOK), :])

    def after_cross(step, rows):
        for half in range(2):
            send_part(give_e2, 0, 2 * step + half, e2_ref, 0)

    attend_back(
        cqh_ref[...], memh_ref[:, 0:PAIR], memh_ref[:, PAIR : 2 * PAIR], do2h_ref, mix2_ref,
        inv2_ref, False, after_cross,
    )
    keeps = [keep_part(0, e2_ref, 0, 2)]
    sums_ref[:, PAIR : 2 * PAIR] = dkt_ref[...].T.astype(LOW)
    sums_ref[:, 2 * PAIR : 3 * PAIR] = dvt_ref[...].T.astype(LOW)
    for there in range(SEQ):
        send_part(give_k2, 1, there, dkv_ref, 0)
        send_part(give_v2, 2, there, dkv_ref, WIDTH)
    keeps += [keep_part(1, dkv_ref, 0, 3), keep_part(2, dkv_ref, WIDTH, 4)]
    exp1_load = load(exp1_hbm, exp_ref, 21)

    keeps[0].wait()
    later[0].wait()
    unit2, inverse2 = norm_unit(x1_ref[...])
    give_e2.receive(from_peers(e2_ref, 0))
    dn2 = dot_nt(e2_ref[...], ring_r[1024:2048, :])
    dx1 = acc_ref[...] + norm_back(dn2, unit2, inverse2, gain_ref[1:2, :])
    acc_ref[...] = dx1
    da_ref[...] = dx1.astype(LOW)
    later[1].wait()
    keep_do1 = push_heads(
        give_do1, do1_ref, lambda rows: ring_r[rows, :], da_ref[...], do1h_ref, 5
    )
    gather.third()
    share(give_be2, e2_ref, b_e2, PAIR)
    share(give_da, da_ref, b_da, PAIR)
    col_n3.finish()
    both_cores(a_n3)
    for one in gathered:
        one.wait()
    both_cores(a_cot)
    both_cores(a_mem)
    for whole in (a_n2, a_o1):
        for step in (-1, 0, 1):
            block_to_core(whole, step)
    vec_ref[1:2, :] = column_sum(dn2 * unit2)
    vec_ref[4:5, :] = column_sum(dn2)
    vec_ref[8:9, :] = column_sum(da_ref[...].astype(F32))
    vec_ref[9:10, :] = column_sum(e2_ref[...].astype(F32))
    keeps[1].wait()
    keeps[2].wait()
    give_k2.receive(from_peers(dkv_ref, 0))
    give_v2.receive(from_peers(dkv_ref, WIDTH))
    share(give_kv, dkv_ref, b_kv, 256)
    later[2].wait()
    gmem_ref[...] = dot_nt(dkv_ref[...], ring_e[...])
    vec_ref[10:11, :] = column_sum(dkv_ref[:, WIDTH : 2 * WIDTH].astype(F32))
    last = [
        load(qkv_hbm.at[:, 0 : 2 * WIDTH], ring_e, 22),
        load(qkv_hbm.at[:, 2 * WIDTH : 3 * WIDTH], ring_r.at[0:1024, :], 23),
    ]

    for index in (0, 1):
        to_core[index][1].wait_recv()
    give_act.receive(lambda to: act_in.at[aligned(to, TOK), :])
    give_dfe.receive(lambda to: dfe_in.at[aligned(to, TOK), :])
    lax.fori_loop(0, 8, fill_f, 0)
    fill_reduce()
    next(run_f)
    col_o2.second()
    col_n2.forward()
    col_o1.forward()

    for exchange in (give_e2, give_k2, give_v2):
        exchange.drain()
    for one in kept1:
        one.wait()
    exp1_load.wait()
    keep_do1.wait()
    give_do1.receive(lambda sender: do1h_ref.at[aligned(sender, TOK), :])

    def after_self(step, rows):
        sums_ref[rows, PAIR : 2 * PAIR] = dkt_ref[:, rows].T.astype(LOW)
        sums_ref[rows, 2 * PAIR : 3 * PAIR] = dvt_ref[:, rows].T.astype(LOW)
        for half in range(2):
            for part, exchange in enumerate((give_q1, give_k1, give_v1)):
                send_part(exchange, part, 2 * step + half, e1_ref, part * WIDTH)

    attend_back(
        heads_ref[:, 0:PAIR], heads_ref[:, PAIR : 2 * PAIR], heads_ref[:, 2 * PAIR : 3 * PAIR],
        do1h_ref, mix1_ref, inv1_ref, True, after_self,
    )
    keeps = [keep_part(part, e1_ref, part * WIDTH, 6 + part) for part in range(3)]
    next(run_f)


    gather.finish()
    for part in range(3):
        value = sums_ref[:, part * PAIR : part * PAIR + PAIR].T
        weight_ref[:, :, :, part * PAIR : part * PAIR + PAIR] = (
            dot(value, n1_all[...]).T.astype(LOW).reshape(DP // 2, 2, ROW // DP, PAIR)
        )
    both_sums = pltpu.make_async_remote_copy(
        src_ref=weight_ref.at[:, 1 - core],
        dst_ref=weight_in.at[0],
        send_sem=pair_send.at[6],
        recv_sem=pair_recv.at[6],
        device_id=place.other,
        device_id_type=MESH,
    )
    both_sums.start()
    pair = dp // 2

    def pair_copy(source, target, distance):
        there = lax.rem(pair + distance + 8, 8)
        return pltpu.make_async_remote_copy(
            src_ref=source.at[there],
            dst_ref=target.at[1, pair],
            send_sem=dp_send.at[distance],
            recv_sem=dp_recv.at[distance],
            device_id=(there * 2 + core, me),
            device_id_type=MESH,
        )

    def pair_receive(target, distance):
        sender = lax.rem(pair - distance + 8, 8)
        return pltpu.make_async_remote_copy(
            src_ref=target.at[1, sender],
            dst_ref=target.at[1, sender],
            send_sem=dp_send.at[distance],
            recv_sem=dp_recv.at[distance],
            device_id=(sender * 2 + core, me),
            device_id_type=MESH,
        )

    def dp_copy(source, target, distance, base):
        there = lax.rem(dp + distance, DP)
        return pltpu.make_async_remote_copy(
            src_ref=source.at[there],
            dst_ref=target.at[dp],
            send_sem=dp_send.at[base + distance],
            recv_sem=dp_recv.at[base + distance],
            device_id=(there, me),
            device_id_type=MESH,
        )

    def dp_receive(target, distance, base):
        sender = lax.rem(dp - distance + DP, DP)
        return pltpu.make_async_remote_copy(
            src_ref=target.at[sender],
            dst_ref=target.at[sender],
            send_sem=dp_send.at[base + distance],
            recv_sem=dp_recv.at[base + distance],
            device_id=(sender, me),
            device_id_type=MESH,
        )

    both_sums.wait()
    weight_sum[...] = (
        weight_ref[:, core].astype(F32) + weight_in[0].astype(F32)
    ).astype(LOW)
    for one in keeps:
        one.wait()
    give_q1.receive(from_peers(e1_ref, 0))
    give_k1.receive(from_peers(e1_ref, WIDTH))
    next(run_f)
    for step in (-1, 0, 1):
        block_to_core(a_o2, step)
    for column, whole in ((col_o2, a_o2), (col_n2, a_n2), (col_o1, a_o1)):
        column.far()
        block_to_core(whole, 2)
    for distance in range(1, 8):
        pair_copy(weight_sum, weight_in, distance).start()

    for one in last:
        one.wait()
    unit1, inverse1 = norm_unit(tok_ref[...].astype(F32))
    dn1 = dot_nt(e1_ref[:, 0 : 2 * WIDTH], ring_e[...])
    give_v1.receive(from_peers(e1_ref, 2 * WIDTH))
    dn1 = dn1 + dot_nt(e1_ref[:, 2 * WIDTH : 3 * WIDTH], ring_r[0:1024, :])
    gtok_ref[...] = acc_ref[...] + norm_back(dn1, unit1, inverse1, gain_ref[0:1, :])
    vec_ref[0:1, :] = column_sum(dn1 * unit1)
    vec_ref[3:4, :] = column_sum(dn1)
    vec_ref[6:7, :] = column_sum(e1_ref[:, 0:WIDTH].astype(F32))
    vec_ref[7:8, :] = column_sum(e1_ref[:, 2 * WIDTH : 3 * WIDTH].astype(F32))

    to_core[2][1].wait_recv()
    for _, arrival in blocks_to_core:
        arrival.wait_recv()
    for exchange, target in ((give_dc, b_dc), (give_be2, b_e2), (give_kv, b_kv), (give_da, b_da)):
        exchange.receive(lambda to, target=target: target.at[aligned(to, TOK), :])
    fill_c()
    next(run_c)

    vec_out[...] = jnp.zeros_like(vec_out)
    for owner in range(DP):
        vec_out[owner, 0:13, 0:64] = vec_ref[0:13, owner * 64 : owner * 64 + 64]
        for half in range(2):
            at = (owner // 8) * 256 + half * PAIR
            vec_out[owner, 13 + half : 14 + half, :] = expand_sums[owner % 8, :, at : at + PAIR]
    for distance in range(1, DP):
        dp_copy(vec_out, vec_in, distance, DP).start()

    next(run_f)
    keeps_f = join(join_f, grads_f, piece_f, 9, True)
    joined(join_f, piece_f, keeps_f)
    gather_f.first()
    next(run_c)
    gather_f.second()
    for distance in range(1, 8):
        pair_receive(weight_in, distance).wait_recv()
    total = weight_sum[pair].astype(F32)
    for distance in range(1, 8):
        total = total + weight_in[1, lax.rem(pair + distance, 8)].astype(F32)
    piece_q[...] = total.astype(LOW)
    next(run_c)
    keeps_c = join(join_c, grads_c, piece_c, 11, False)
    spread(piece_q, all_q, 70, 12)
    gather_f.third()
    for distance in range(1, DP):
        dp_receive(vec_in, distance, DP).wait_recv()
    total = vec_out[dp]
    for distance in range(1, DP):
        total = total + vec_in[lax.rem(dp + distance, DP)]
    piece_v[...] = total
    spread(piece_v, all_v, 86, 14)
    joined(join_c, piece_c, keeps_c)
    spread(piece_c, all_c, 94, 15)
    gather_f.finish()

    for exchange, keep, whole in spreads:
        keep.wait()
        exchange.receive(lambda sender, whole=whole: whole.at[sender])
        exchange.drain()
    for exchange in (give_do2, give_do1, give_q1, give_k1, give_v1):
        exchange.drain()
    for copy, _ in to_core + blocks_to_core:
        copy.wait_send()
    col_o2.sent_near()
    for exchange in (give_act, give_dfe, give_dc, give_be2, give_kv, give_da, join_f, join_c):
        exchange.drain()
    for distance in range(1, DP):
        dp_copy(vec_out, vec_in, distance, DP).wait_send()
    for distance in range(1, 8):
        pair_copy(weight_sum, weight_in, distance).wait_send()
    sum_f.drain()
    sum_c.drain()


def back_call(operands):
    dma = pltpu.SemaphoreType.DMA
    vmem = pltpu.VMEM
    token = vmem((TOK, WIDTH), LOW)
    token_wide = vmem((TOK, WIDTH), F32)
    heads = vmem((ROW, PAIR), LOW)
    inverse = vmem((ROW, PAIR), F32)
    eight = vmem((4, 2, TOK, WIDTH), LOW)
    column = vmem((ROW, PAIR), LOW)
    chunk = vmem((ROW, FF_CHUNK), LOW)
    chunks = vmem((7, TOK, FF_CHUNK), LOW)

    def sums(rows, lanes):
        return [
            vmem((4, 4, rows, lanes), LOW), vmem((3, 4, rows, lanes), LOW),
            vmem((3, rows, lanes), LOW),
        ]

    return pl.pallas_call(
        back_kernel,
        out_shape=(
            shaped((TOK, WIDTH)), shaped((TOK, WIDTH), F32), shaped((TOK, WIDTH), F32),
            shaped((SEQ, 256, LANES)), shaped((SEQ, 128, 384)),
            shaped((SEQ, 64, 3 * PAIR)), shaped((SEQ, 16, PAIR), F32),
        ),
        in_specs=[spec_vmem()] * 3 + [spec_any()] * 25,
        out_specs=(spec_vmem(),) * 4 + (spec_any(),) * 3,
        scratch_shapes=[
            vmem((ROW, WIDTH), LOW),
            vmem((WIDTH, 2 * WIDTH), LOW), vmem((2 * WIDTH, WIDTH), LOW), vmem((WIDTH, WIDTH), LOW),
            vmem((2, ROW, ROW), LOW), token_wide, token, token,
            vmem((ROW, 3 * PAIR), LOW), vmem((ROW, 2 * PAIR), LOW), heads, heads, heads, inverse,
            inverse,
            eight, eight, eight, eight, eight, eight, chunk, chunk, chunks, chunks,
            column, column, column, vmem((ROW, 256), LOW),
            token, token, token_wide, token_wide,
            vmem((FF // FF_CHUNK, 1, FF_CHUNK), F32), vmem((16, WIDTH), F32),
            token, token, heads, heads, vmem((ROW, 3 * PAIR), LOW), token,
            vmem((TOK, 2 * WIDTH), LOW), vmem((TOK, 3 * WIDTH), LOW),
            vmem((PAIR, ROW), F32), vmem((PAIR, ROW), F32),
        ]
        + sums(256, LANES) + sums(128, 384)
        + [
            vmem((256, LANES), LOW), vmem((128, 384), LOW),
            vmem((8, 2, 64, 3 * PAIR), LOW), vmem((2, 8, 64, 3 * PAIR), LOW),
            vmem((8, 64, 3 * PAIR), LOW),
            vmem((64, 3 * PAIR), LOW), vmem((DP, 16, PAIR), F32), vmem((DP, 16, PAIR), F32),
            vmem((16, PAIR), F32),
            dma((38,)), dma((16,)), dma((16,)), dma((19,)), dma((19,)), dma((102,)), dma((102,)),
            dma((32,)), dma((32,)), dma((48,)), dma((48,)), dma((64,)), dma((64,)), dma((16,)),
            dma((16,)),
        ],
        compiler_params=pltpu.CompilerParams(
            collective_id=3, has_side_effects=True, vmem_limit_bytes=63 * MIB
        ),
        cost_estimate=pl.CostEstimate(
            flops=2 * TOK * WIDTH * 27 * WIDTH, bytes_accessed=100 * MIB, transcendentals=0
        ),
        name="back",
    )(*operands)


def finish_kernel(
    f_hbm, c_hbm, q_hbm, vec_hbm, output_hbm, gtok_hbm, gmem_hbm,
    gqkv_ref, gout_ref, gque_ref, gckv_ref, gcro_ref, gexp_ref, gred_ref, ggain_ref, gbias_ref,
    gebias_ref, to_output, to_gtok, to_gmem,
    f_ref, c_ref, q_ref, vec_ref, sems,
):
    copies = [
        pltpu.make_async_copy(source, target, sems.at[index])
        for index, (source, target) in enumerate(
            (
                (f_hbm, f_ref), (c_hbm, c_ref), (q_hbm, q_ref), (vec_hbm, vec_ref),
                (output_hbm, to_output), (gtok_hbm, to_gtok), (gmem_hbm, to_gmem),
            )
        )
    ]
    for one in copies:
        one.start()
    for one in copies[:4]:
        one.wait()
    for seq in range(SEQ):
        y, xl = seq // 2, seq % 2
        rows = slice(16 * y, 16 * y + 16)
        for owner in range(8):
            own = slice(owner * 16, owner * 16 + 16)
            at = (owner + 8 * xl) * 256
            gexp_ref[rows, at : at + 256] = f_ref[seq, own, :].astype(F32)
            if xl == 0:
                for index, target in enumerate((gque_ref, gout_ref, gcro_ref)):
                    target[rows, owner * PAIR : owner * PAIR + PAIR] = c_ref[
                        seq, own, index * PAIR : index * PAIR + PAIR
                    ].astype(F32)
            else:
                gckv_ref[rows, owner * 256 : owner * 256 + 256] = c_ref[seq, own, 0:256].astype(F32)
        for sub in range(2):
            at = xl * 512 + sub * LANES
            gred_ref[64 * y : 64 * y + 64, at : at + LANES] = f_ref[
                seq, 128 + sub * 64 : 192 + sub * 64, :
            ].astype(F32)
        for part in range(3):
            at = part * WIDTH + seq * PAIR
            gqkv_ref[:, at : at + PAIR] = q_ref[seq, :, part * PAIR : (part + 1) * PAIR].astype(F32)
    total = vec_ref[0]
    for seq in range(1, SEQ):
        total = total + vec_ref[seq]
    ggain_ref[...] = total[0:3, 0:64]
    gbias_ref[...] = total[3:13, 0:64]
    gebias_ref[:, 0:PAIR] = total[13:14, :]
    gebias_ref[:, PAIR : 2 * PAIR] = total[14:15, :]
    for one in copies[4:]:
        one.wait()


def finish_call(operands):
    vmem = pltpu.VMEM
    return pl.pallas_call(
        finish_kernel,
        out_shape=(
            shaped((64, 3 * WIDTH), F32), shaped((64, WIDTH), F32), shaped((64, WIDTH), F32),
            shaped((64, 2 * WIDTH), F32), shaped((64, WIDTH), F32), shaped((64, FF), F32),
            shaped((256, WIDTH), F32), shaped((3, 64), F32), shaped((10, 64), F32),
            shaped((1, 256), F32), shaped((TOK, WIDTH)), shaped((TOK, WIDTH), F32),
            shaped((TOK, WIDTH), F32),
        ),
        in_specs=[spec_any()] * 7,
        out_specs=(spec_vmem(),) * 13,
        scratch_shapes=[
            vmem((SEQ, 256, LANES), LOW), vmem((SEQ, 128, 384), LOW), vmem((SEQ, 64, 3 * PAIR), LOW),
            vmem((SEQ, 16, PAIR), F32), pltpu.SemaphoreType.DMA((8,)),
        ],
        compiler_params=pltpu.CompilerParams(vmem_limit_bytes=63 * MIB),
        cost_estimate=pl.CostEstimate(flops=0, bytes_accessed=10 * MIB, transcendentals=0),
        name="finish",
    )(*operands)


def on_device(
    tokens, memory, cotangent, offsets, memory_ids, pair_map, self_qkv, self_out, cross_query,
    cross_kv, cross_out, expand_weight, expand_bias, reduce_weight, norm_gains, bias_rows,
):
    tok = tokens.reshape(TOK, WIDTH)
    mem = memory.reshape(TOK, WIDTH)
    cot = cotangent.reshape(TOK, WIDTH)
    (
        x1, _, _, o2, heads, mem_heads, cq, mix1, mix2, inv1, inv2, n1, exp1, exp2, cot4, mem4, n24, o14,
    ) = front_call(
        (tok, mem, cot, norm_gains, bias_rows, memory_ids, offsets, pair_map, self_qkv, cross_kv,
         self_out, cross_query)
    )
    output, gtok, gmem, all_f, all_c, all_q, all_v = back_call(
        (norm_gains, bias_rows, expand_bias.reshape(1, FF),
         o2, x1, cot, tok, n1, cot4, mem4, n24, o14, heads, mem_heads, cq, mix1, mix2, inv1, inv2,
         exp1, exp2, self_qkv, cross_kv, self_out, cross_query, cross_out, expand_weight,
         reduce_weight)
    )
    (
        gqkv, gout, gque, gckv, gcro, gexp, gred, ggain, gbias, gebias, output, gtok, gmem,
    ) = finish_call((all_f, all_c, all_q, all_v, output, gtok, gmem))
    return (
        output.reshape(1, TOK, WIDTH), gtok.reshape(1, TOK, WIDTH), gmem.reshape(1, TOK, WIDTH),
        gqkv, gout, gque, gckv, gcro, gexp, gebias.reshape(256), gred, ggain, gbias,
    )


def solution(mesh):
    row = P("dp", "seq", None)
    split = P("dp", None)
    in_specs = (row,) * 3 + (split,) * 3 + (P(),) * 10
    out_specs = (row,) * 3 + (split,) * 6 + (P("dp"), split, P(None, "dp"), P(None, "dp"))
    return jax.shard_map(
        on_device, mesh=mesh, in_specs=in_specs, out_specs=out_specs, check_vma=False
    )
```

profile of v0, /device:TPU:0, one launch (start us, length us, event | category | flops | bytes accessed | tf_op | source)
XLA Modules:
  0.0 172.7 jit_solution(12325491954133921461)
XLA Ops:
  0.6 47.5 %front.1 = (f32[128,1024]{1,0:T(8,128)}, bf16[128,1024]{1,0:T(8,128)(2,1)}, bf16[128,1024]{1,0:T(8,128)(2,1)}, bf16[128,1024]{1,0:T(8,128)(2,1)}, bf16[1024,384]...) custom-call(bf16[128,1024]{1,0:T(8,128)(2,1)} %bitcast.8, ...), custom_call_target="tpu_custom_call" | custom-call | flops 1879048192 | bytes 62914560 | tf_op jit(solution)/shard_map/front/pallas_call | solution.py:517
  48.2 119.5 %back.1 = (bf16[128,1024]{1,0:T(8,128)(2,1)}, f32[128,1024]{1,0:T(8,128)}, f32[128,1024]{1,0:T(8,128)}, bf16[8,256,256]{2,1,0:T(8,128)(2,1)}, bf16[8,128,384]{2,...) custom-call(f32[3,1024]{1,0:T(4,128)} %gain_ref.3, f32[10,1024]{1,0:T(8,128)} %bias_ref.3, ...), custom_call_target="tpu_custom_call" | custom-call | flops 7247757312 | bytes 104857600 | tf_op jit(solution)/shard_map/back/pallas_call | solution.py:1401
  167.7 4.5 %finish.1 = (f32[64,3072]{1,0:T(8,128)}, f32[64,1024]{1,0:T(8,128)}, f32[64,1024]{1,0:T(8,128)}, f32[64,2048]{1,0:T(8,128)}, f32[64,1024]{1,0:T(8,128)}, /*index...) custom-call(bf16[8,256,256]{2,1,0:T(8,128)(2,1)} %get-tuple-element., ...), custom_call_target="tpu_custom_call" | custom-call | bytes 10485760 | tf_op jit(solution)/shard_map/finish/pallas_call | solution.py:1499
where the time goes:
time: 176 us; the launch traced here: 173 us
  Pallas kernels  172 us (98%)
    pallas_call x1, Pallas kernels, back_call(): pl.pallas_call(back_kernel, out_shape=(shaped((TOK, WIDTH)), shaped((TOK,...  120 us
    pallas_call x1, Pallas kernels, front_call(): pl.pallas_call(front_kernel, out_shape=(shaped((TOK, WIDTH), F32), token,...  47.5 us
    pallas_call x1, Pallas kernels, finish_call(): pl.pallas_call(finish_kernel, out_shape=(shaped((64, 3 * WIDTH), F32), sh...  4.49 us

commit v1 on v0

--- a/solution.py
+++ b/solution.py
@@ -319,8 +319,9 @@
 def front_kernel(
     tok_ref, mem_ref, cot_ref, gain_ref, bias_ref, ids_ref, offsets_ref, pair_ref,
     qkv_hbm, ckv_hbm, out_hbm, query_hbm,
-    x1_ref, n2_ref, o1_ref, o2_ref, heads_ref, memh_ref, cqh_ref, mix1_ref, mix2_ref,
-    inv1_ref, inv2_ref, n1_ref, exp1_hbm, exp2_hbm, cot_all, mem_all, n2_all, o1_all,
+    o2_ref, mix2_ref, inv2_ref, x1_hbm, heads_hbm, memh_hbm, cqh_hbm, mix1_hbm, inv1_hbm, n1_hbm,
+    exp1_hbm, exp2_hbm, cot_all, mem_all, n2_all, o1_all,
+    x1_ref, n2_ref, o1_ref, heads_ref, memh_ref, cqh_ref, mix1_ref, inv1_ref, n1_ref,
     qkv_w, ckv_w, out_w, query_w, give_heads, give_mem, cq_ref, exp1_ref, exp2_ref,
     load_sems, keep_sems, exp_sems, send_sems, recv_sems,
 ):
@@ -369,6 +370,14 @@
     unit, _ = norm_unit(tok_ref[...].astype(F32))
     n1 = (unit * gain_ref[0:1, :] + bias_ref[0:1, :]).astype(LOW)
     n1_ref[...] = n1
+    stored = []
+
+    def store(source, target):
+        copy = pltpu.make_async_copy(source, target, keep_sems.at[11 + len(stored)])
+        copy.start()
+        stored.append(copy)
+
+    store(n1_ref, n1_hbm)
     mem = mem_ref[...]
     for kind, count, source, give, heads, exchange in (
         ("qkv", 3, n1, give_heads, heads_ref, give_qkv),
@@ -444,6 +453,7 @@
 
     loads["qkv"].wait()
     give_qkv.receive(lambda sender: heads_ref.at[aligned(sender, TOK), :])
+    store(heads_ref, heads_hbm)
     key_t = heads_ref[:, PAIR : 2 * PAIR].T
     keep1 = attended(
         lambda step, width: self_allowed(offsets_ref, step, 256, width),
@@ -452,12 +462,15 @@
     )
     columns[0].second()
     columns[1].second()
+    store(mix1_ref, mix1_hbm)
+    store(inv1_ref, inv1_hbm)
     keep1.wait()
     loads["out"].wait()
     back1.receive(lambda sender: o1_ref.at[:, aligned(sender, PAIR)])
     columns[2].first()
     x1 = tok_ref[...].astype(F32) + dot(o1_ref[...], out_w[...]) + bias_ref[5:6, :]
     x1_ref[...] = x1
+    store(x1_ref, x1_hbm)
     unit, _ = norm_unit(x1)
     n2 = (unit * gain_ref[1:2, :] + bias_ref[1:2, :]).astype(LOW)
     n2_ref[...] = n2
@@ -476,9 +489,11 @@
     keep.start()
     loads["ckv"].wait()
     give_kv.receive(lambda sender: memh_ref.at[aligned(sender, TOK), :])
+    store(memh_ref, memh_hbm)
     key_t = memh_ref[:, 0:PAIR].T
     keep.wait()
     give_q.receive(lambda sender: cqh_ref.at[aligned(sender, TOK), :])
+    store(cqh_ref, cqh_hbm)
     ids = ids_ref[...]
     keep2 = attended(
         lambda step, width: cross_allowed(ids, offsets_ref, pair_ref, step, 256),
@@ -498,6 +513,8 @@
             pltpu.make_async_copy(
                 exp2_ref.at[spot], exp2_hbm.at[spot], exp_sems.at[8 + step * 2 + head]
             ).wait()
+    for one in stored:
+        one.wait()
     for exchange in (give_qkv, give_kv, back1, give_q, back2):
         exchange.drain()
     for column in columns[:2]:
@@ -517,17 +534,19 @@
     return pl.pallas_call(
         front_kernel,
         out_shape=(
-            shaped((TOK, WIDTH), F32), token, token, token, shaped((ROW, 3 * PAIR)),
-            shaped((ROW, 2 * PAIR)), heads, heads, heads, inverse, inverse, token,
-            exps, exps, four, four, four, four,
+            token, heads, inverse, shaped((TOK, WIDTH), F32), shaped((ROW, 3 * PAIR)),
+            shaped((ROW, 2 * PAIR)), heads, heads, inverse, token, exps, exps, four, four, four, four,
         ),
         in_specs=[spec_vmem()] * 6 + [spec_smem()] * 2 + [spec_any()] * 4,
-        out_specs=(spec_vmem(),) * 12 + (spec_any(),) * 6,
+        out_specs=(spec_vmem(),) * 3 + (spec_any(),) * 13,
         scratch_shapes=[
+            vmem((TOK, WIDTH), F32), vmem((TOK, WIDTH), LOW), vmem((TOK, WIDTH), LOW),
+            vmem((ROW, 3 * PAIR), LOW), vmem((ROW, 2 * PAIR), LOW), vmem((ROW, PAIR), LOW),
+            vmem((ROW, PAIR), LOW), vmem((ROW, PAIR), F32), vmem((TOK, WIDTH), LOW),
             vmem((WIDTH, 3 * WIDTH), LOW), vmem((WIDTH, 2 * WIDTH), LOW), vmem((WIDTH, WIDTH), LOW),
             vmem((WIDTH, WIDTH), LOW), vmem((SEQ, TOK, 3 * PAIR), LOW), vmem((SEQ, TOK, 2 * PAIR), LOW),
             vmem((TOK, WIDTH), LOW), vmem((2, ROW, ROW), LOW), vmem((2, ROW, ROW), LOW),
-            dma((22,)), dma((11,)), dma((16,)), dma((56,)), dma((56,)),
+            dma((22,)), dma((18,)), dma((16,)), dma((56,)), dma((56,)),
         ],
         compiler_params=pltpu.CompilerParams(
             collective_id=2, has_side_effects=True, vmem_limit_bytes=56 * MIB
@@ -1525,7 +1544,7 @@
     mem = memory.reshape(TOK, WIDTH)
     cot = cotangent.reshape(TOK, WIDTH)
     (
-        x1, _, _, o2, heads, mem_heads, cq, mix1, mix2, inv1, inv2, n1, exp1, exp2, cot4, mem4, n24, o14,
+        o2, mix2, inv2, x1, heads, mem_heads, cq, mix1, inv1, n1, exp1, exp2, cot4, mem4, n24, o14,
     ) = front_call(
         (tok, mem, cot, norm_gains, bias_rows, memory_ids, offsets, pair_map, self_qkv, cross_kv,
          self_out, cross_query)

time: 176 us -> 174 us (0.989)
  Pallas kernels: 172 us -> 170 us
where the time goes in v1:
time: 174 us; the launch traced here: 171 us
  Pallas kernels  170 us (98%)
    pallas_call x1, Pallas kernels, back_call(): pl.pallas_call(back_kernel, out_shape=(shaped((TOK, WIDTH)), shaped((TOK,...  119 us
    pallas_call x1, Pallas kernels, front_call(): pl.pallas_call(front_kernel, out_shape=(token, heads, inverse, shaped((TO...  46.4 us
    pallas_call x1, Pallas kernels, finish_call(): pl.pallas_call(finish_kernel, out_shape=(shaped((64, 3 * WIDTH), F32), sh...  4.49 us

profile of v1, /device:TPU:0, one launch (start us, length us, event | category | flops | bytes accessed | tf_op | source)
XLA Modules:
  0.0 171.5 jit_solution(10264912998556110318)
XLA Ops:
  0.6 46.4 %front.1 = (bf16[128,1024]{1,0:T(8,128)(2,1)}, bf16[1024,128]{1,0:T(8,128)(2,1)}, f32[1024,128]{1,0:T(8,128)}, f32[128,1024]{1,0:T(8,128)}, bf16[1024,384]{1,0:T...) custom-call(bf16[128,1024]{1,0:T(8,128)(2,1)} %bitcast.8, ...), custom_call_target="tpu_custom_call" | custom-call | flops 1879048192 | bytes 62914560 | tf_op jit(solution)/shard_map/front/pallas_call | solution.py:534
  47.0 119.5 %back.1 = (bf16[128,1024]{1,0:T(8,128)(2,1)}, f32[128,1024]{1,0:T(8,128)}, f32[128,1024]{1,0:T(8,128)}, bf16[8,256,256]{2,1,0:T(8,128)(2,1)}, bf16[8,128,384]{2,...) custom-call(f32[3,1024]{1,0:T(4,128)} %gain_ref.3, f32[10,1024]{1,0:T(8,128)} %bias_ref.3, ...), custom_call_target="tpu_custom_call" | custom-call | flops 7247757312 | bytes 104857600 | tf_op jit(solution)/shard_map/back/pallas_call | solution.py:1420
  166.5 4.5 %finish.1 = (f32[64,3072]{1,0:T(8,128)}, f32[64,1024]{1,0:T(8,128)}, f32[64,1024]{1,0:T(8,128)}, f32[64,2048]{1,0:T(8,128)}, f32[64,1024]{1,0:T(8,128)}, /*index...) custom-call(bf16[8,256,256]{2,1,0:T(8,128)(2,1)} %get-tuple-element., ...), custom_call_target="tpu_custom_call" | custom-call | bytes 10485760 | tf_op jit(solution)/shard_map/finish/pallas_call | solution.py:1518
